TPU v7x, 32 devices: a whole 2x2x4 slice. The times are simulated.
32 devices in a mesh: group: 2 (over x), dx: 16 (over z, y, core).
Axes of the slice: x: 2, y: 2, z: 4, core: 2. Of those that a mesh axis runs over, the one named last changes fastest.
Arguments:
- points: bfloat16 [16384, 1024], P(('group', 'dx')), parts along dimension 0, may hold values from -6 to 6
- cotangent: bfloat16 [16384, 1024], P(('group', 'dx')), parts along dimension 0, may hold values from -96 to 96
- counts: int32 [32], P(('group', 'dx')), parts along dimension 0, may hold values from 170 to 512, as said below
- w_query: bfloat16 [1024, 1024], replicated, may hold values from -0.1875 to 0.1875
- w_key: bfloat16 [1024, 1024], replicated, may hold values from -0.1875 to 0.1875
- w_value: bfloat16 [1024, 1024], replicated, may hold values from -0.1875 to 0.1875
- gain_key: float32 [1024], replicated, may hold values from 0.25 to 1.75
- bias_key: float32 [1024], replicated, may hold values from -3 to 3
- gain_value: float32 [1024], replicated, may hold values from 0.25 to 1.75
- bias_value: float32 [1024], replicated, may hold values from -3 to 3
Outputs:
- grad_points: bfloat16 [16384, 1024], P(('group', 'dx')), parts along dimension 0
There are 2 independent parts, one for each index of `group`. A program takes and returns all parts, laid end to end along the dimension named above; an argument that names none is the same for every part. Nothing has to cross between parts.
Inputs may be any that keep to these rules, and one draw needn't show every extreme that they name: `counts`: live points of each tile; some tile of every slab holds 512.
All inputs are finite; a program needn't handle non-finite values.
Results may differ from a plain program's by a relative error of at most 0.006.
Values sent between devices are 32-bit elements; how exact they have to be, the bound alone decides.
A program may use at most 64 MiB of HBM per device.

v0:
```python
import jax
import jax.numpy as jnp
from jax import lax
from jax.sharding import PartitionSpec as P

HEADS = 8
eps = 1e-05


def head_norm(raw, heads):
    grouped = raw.reshape(raw.shape[0], heads, -1)
    center = grouped - jnp.mean(grouped, axis=2, keepdims=True)
    inverse = lax.rsqrt(jnp.mean(center * center, axis=2, keepdims=True) + eps)
    return (center * inverse, inverse)


def norm_back(grad, gain, normed, inverse, heads):
    scaled = grad * gain.reshape(heads, -1)
    inner = scaled - jnp.mean(scaled, axis=2, keepdims=True)
    inner = inner - normed * jnp.mean(scaled * normed, axis=2, keepdims=True)
    return (inverse * inner).reshape(grad.shape[0], -1).astype(jnp.bfloat16)


def body(
    points, cotangent, counts, w_query, w_key, w_value, gain_key, bias_key, gain_value, bias_value
):
    rows = points.shape[0]
    heads = HEADS
    live = (lax.iota(jnp.int32, rows) < counts[0]).astype(jnp.float32)[:, None]
    live_h = live[:, :, None]
    own_count = counts[0].astype(jnp.float32)
    total = lax.psum(own_count, "dx")
    key_hat, key_inv = head_norm(jnp.dot(points, w_key, preferred_element_type=jnp.float32), heads)
    value_hat, value_inv = head_norm(
        jnp.dot(points, w_value, preferred_element_type=jnp.float32), heads
    )
    keys = (live_h * (key_hat * gain_key.reshape(heads, -1) + bias_key.reshape(heads, -1))).astype(
        jnp.bfloat16
    )
    values = (
        live_h * (value_hat * gain_value.reshape(heads, -1) + bias_value.reshape(heads, -1))
    ).astype(jnp.bfloat16)
    kv_local = jnp.einsum("nhi,nhj->hij", keys, values, preferred_element_type=jnp.float32)
    cot = cotangent.reshape(rows, heads, -1)
    kv_sum = lax.psum(kv_local, "dx")
    query = jnp.dot(points, w_query, preferred_element_type=jnp.float32).astype(jnp.bfloat16)
    masked_query = (query * live.astype(jnp.bfloat16)).reshape(rows, heads, -1)
    qdy_local = jnp.einsum("nhi,nhj->hij", masked_query, cot, preferred_element_type=jnp.float32)
    qdy_sum = lax.psum(qdy_local, "dx")
    gram = (kv_sum / total).astype(jnp.bfloat16)
    dgram = (qdy_sum / total).astype(jnp.bfloat16)
    dquery = (
        (live_h * jnp.einsum("nhj,hij->nhi", cot, gram, preferred_element_type=jnp.float32))
        .reshape(rows, -1)
        .astype(jnp.bfloat16)
    )
    dkeys = jnp.einsum("nhj,hij->nhi", values, dgram, preferred_element_type=jnp.float32)
    dvalues = jnp.einsum("nhi,hij->nhj", keys, dgram, preferred_element_type=jnp.float32)
    dkey_raw = norm_back(dkeys, gain_key, key_hat, key_inv, heads)
    dvalue_raw = norm_back(dvalues, gain_value, value_hat, value_inv, heads)
    grad = jnp.dot(dquery, w_query.T, preferred_element_type=jnp.float32)
    grad = grad + jnp.dot(dkey_raw, w_key.T, preferred_element_type=jnp.float32)
    grad = grad + jnp.dot(dvalue_raw, w_value.T, preferred_element_type=jnp.float32)
    return grad.astype(jnp.bfloat16)


def solution(mesh):
    placed = (
        P(("group", "dx"), None),
        P(("group", "dx"), None),
        P(("group", "dx")),
        P(),
        P(),
        P(),
        P(),
        P(),
        P(),
        P(),
    )
    return jax.shard_map(
        body, mesh=mesh, in_specs=placed, out_specs=P(("group", "dx"), None), check_vma=False
    )
```

profile of v0, /device:TPU:0, one launch (start us, length us, event | category | flops | bytes accessed | tf_op | source)
XLA Modules:
  0.0 156.2 jit_solution(9435731812244880489)
XLA Ops:
  6.5 0.0 copy-start
  6.5 0.0 all-reduce.3.cloned.1.call-start
  6.5 3.3 %convolution_bitcast_fusion = f32[64,8,8,128]{3,1,2,0:T(8,128)S(1)} fusion(bf16[512,1024]{1,0:T(8,128)(2,1)} %param.10, bf16[1024,1024]{1,0:T(8,128)(2,1)} %param.15), kind=kOutput, calls=%fused_computation.22 | convolution fusion | flops 1073741824 | bytes 5242880 | tf_op jit(solution)/shard_map/dot_general | solution.py:35
  9.8 1.8 %copy.72 = f32[64,8,8,128]{3,2,1,0:T(8,128)} copy(f32[64,8,8,128]{3,1,2,0:T(8,128)S(1)} %convolution_bitcast_fusion) | data formatting | bytes 4194304
  11.6 3.0 %copy.57 = f32[512,8,128]{0,2,1:T(8,128)} copy(f32[512,8,128]{2,1,0:T(8,128)} %bitcast.70) | data formatting | bytes 4194304 | tf_op jit(solution)/shard_map/reshape | solution.py:11
  14.6 2.3 %reduce_sum.74 = f32[512,8]{1,0:T(8,128)S(1)} reduce(f32[512,8,128]{2,1,0:T(8,128)} %bitcast.71, f32[]{:T(128)} %constant.11.clone.1), dimensions={2}, to_apply=%region_2.0 | reduce | flops 520192 | bytes 2113540 | tf_op jit(solution)/shard_map/reduce_sum | solution.py:12
  16.9 0.0 copy-done
  16.9 0.0 copy-done.11
  16.9 1.3 convolution_bitcast_fusion.1
  18.2 1.8 %copy.71 = f32[64,8,8,128]{3,2,1,0:T(8,128)} copy(f32[64,8,8,128]{3,1,2,0:T(8,128)S(1)} %convolution_bitcast_fusion.1) | data formatting | bytes 4194304
  20.0 2.9 %copy.55 = f32[512,8,128]{0,2,1:T(8,128)} copy(f32[512,8,128]{2,1,0:T(8,128)} %bitcast.68) | data formatting | bytes 4194304 | tf_op jit(solution)/shard_map/reshape | solution.py:11
  22.9 2.2 %reduce_sum.72 = f32[512,8]{1,0:T(8,128)S(1)} reduce(f32[512,8,128]{2,1,0:T(8,128)} %bitcast.69, f32[]{:T(128)} %constant.11.clone.1), dimensions={2}, to_apply=%region_0.0 | reduce | flops 520192 | bytes 2113540 | tf_op jit(solution)/shard_map/reduce_sum | solution.py:12
  25.1 0.1 copy.56
  25.2 0.1 copy.54
  26.0 4.1 %fusion.8 = bf16[512,1024]{1,0:T(8,128)(2,1)} fusion(bf16[512,1024]{1,0:T(8,128)(2,1)} %param.10, bf16[1024,1024]{1,0:T(8,128)(2,1)} %param.13, bf16[512]{0:T(512)(128)(2,1)S(1)} %get-tuple-element.14), kind=kOutput, calls=%fused_computation.25 | convolution fusion | flops 1074790400 | bytes 4195328 | tf_op jit(solution)/shard_map/dot_general | solution.py:46
  30.2 1.5 copy.69
  31.7 0.0 copy-start.3
  31.7 0.0 copy-start.5
  31.7 2.0 %multiply_reduce_fusion = f32[512,8]{0,1:T(8,128)S(1)} fusion(f32[512,8,128]{0,2,1:T(8,128)} %copy.57, f32[512,8]{0,1:T(8,128)S(1)} %broadcast_multiply_fusion.4), kind=kLoop, calls=%fused_computation.17 | loop fusion | flops 1568768 | bytes 2129920 | tf_op jit(solution)/shard_map/reduce_sum | solution.py:13
  33.7 0.2 copy-done.3
  33.9 0.0 copy-start.15
  33.9 0.3 multiply_reduce_fusion.1
  34.2 0.0 copy-done.5
  34.2 1.3 fusion.9
  35.5 0.0 copy-done.1
  35.5 0.0 copy-done.7
  35.5 0.0 copy-done.8
  35.6 0.0 copy-done.14
  35.6 0.0 copy-done.15
  35.6 2.0 %fusion.18 = f32[8,128,128]{2,1,0:T(8,128)} fusion(f32[512,8,128]{0,2,1:T(8,128)S(1)} %copy-done.3, f32[8,128]{1,0:T(8,128)S(1)} %bitcast.83, f32[8,128]{1,0:T(8,128)S(1)} %bitcast.75, f32[512,8]{0,1:T(8,128)S(1)} %get-tuple-element.16, f32[512,8]{0,1:T(8,128)S(1)} %broadcast_multiply_fusion.5, f32[512]{0:T(512)S(1)} %get-tuple-element.13, ...), kind=kOutput, calls=%fused_computation.46 | convolution fusion | flops 140509184 | bytes 4802560 | tf_op jit(solution)/shard_map/nhi,nhj->hij/dot_general | solution.py:43
  37.5 0.0 all-reduce.3.cloned.1.call-update
  37.6 35.9 %psum.22 = f32[]{:T(128)} all-reduce(f32[]{:T(128)S(6)} %convert_element_type.64), channel_id=1, replica_groups=mesh['group'=2,'dx'=16] {'dx'}, use_global_device_ids=true, to_apply=%region_5.0 | all-reduce | flops 1 | bytes 8 | tf_op jit(solution)/shard_map/psum | solution.py:32
  73.5 60.4 %all-reduce.3.cloned.1.call-done = (f32[8,128,128]{2,1,0:T(8,128)}, f32[8,128,128]{2,1,0:T(8,128)}) async-done(((f32[8,128,128]{2,1,0:T(8,128)}, f32[8,128,128]{2,1,0:T(8,128)}), (f32[8,128,128]{2,1,0:T(8,128)}, f32[8,128,128]{2,1,0:T(8,128)})) %all-reduce.3.cloned.1.call-update) | async-done | bytes 1048592 | tf_op jit(solution)/shard_map/psum | solution.py:45
  133.9 4.8 %bitcast_reduce_fusion = (f32[512,8]{0,1:T(8,128)S(1)}, f32[512,8]{0,1:T(8,128)S(1)}, f32[8,128,512]{2,1,0:T(8,128)S(1)}) fusion(f32[8,128]{1,0:T(8,128)S(1)} %bitcast.80, f32[512,8]{0,1:T(8,128)S(1)} %get-tuple-element.15, f32[512,8,128]{0,2,1:T(8,128)} %copy.57, f32[512,8]{0,1:T(8,128)S(1)} %broadcast_multiply_fusion.4, f32[512,8,128]{0,2,1:T(8,128)} %copy.55, ...), kind=kOutput, calls=%fused_computation.2 | convolution fusion | flops 140763136 | bytes 6928388 | tf_op jit(solution)/shard_map/nhi,hij->nhj/dot_general | solution.py:58
  138.7 0.0 copy-done.2
  138.7 0.0 copy-done.4
  138.7 1.7 %bitcast_reduce_fusion.1 = (f32[512,8]{0,1:T(8,128)S(1)}, f32[512,8]{0,1:T(8,128)S(1)}, f32[8,128,512]{2,1,0:T(8,128)S(1)}) fusion(f32[8,128]{1,0:T(8,128)S(1)} %bitcast.77, f32[512,8]{0,1:T(8,128)S(1)} %get-tuple-element.16, f32[512,8,128]{0,2,1:T(8,128)S(1)} %copy-done.4, f32[512,8]{0,1:T(8,128)S(1)} %broadcast_multiply_fusion.5, ...), kind=kOutput, calls=%fused_computation.9 | convolution fusion | flops 140763136 | bytes 6928388 | tf_op jit(solution)/shard_map/nhj,hij->nhi/dot_general | solution.py:57
  140.5 0.8 fusion.6
  141.3 0.0 copy-start.6
  141.3 1.3 fusion.21
  142.6 0.0 copy-start.9
  142.6 1.3 multiply_convert_fusion
  143.9 0.3 copy-done.9
  144.2 1.3 fusion.20
  145.5 0.0 copy-start.10
  145.5 0.8 fusion.2
  146.3 0.8 copy-done.10
  147.1 2.3 %add_convert_fusion = bf16[512,1024]{1,0:T(8,128)(2,1)} fusion(f32[512,1024]{1,0:T(8,128)S(1)} %fusion.20, f32[512,1024]{1,0:T(8,128)S(1)} %fusion.21, bf16[512,1024]{0,1:T(8,128)(2,1)S(1)} %bitcast.73, bf16[1024,1024]{1,0:T(8,128)(2,1)S(1)} %copy-done.10), kind=kOutput, calls=%fused_computation.14 | convolution fusion | flops 1075314688 | bytes 8388608 | tf_op jit(solution)/shard_map/dot_general | solution.py:63
  (20 shorter events, 0.1 us)
Async XLA Ops:
  6.5 10.4 %copy-start = (bf16[1024,1024]{1,0:T(8,128)(2,1)S(1)}, bf16[1024,1024]{1,0:T(8,128)(2,1)}, u32[]{:S(2)}) copy-start(bf16[1024,1024]{1,0:T(8,128)(2,1)} %param.14) | copy-start | bytes 6291460
  6.5 127.3 %all-reduce.3.cloned.1.call-start = ((), (), s32[]{:S(2)}) async-start(), calls=%async_computation | async-start | bytes 2097152 | tf_op jit(solution)/shard_map/psum | solution.py:45
  14.6 2.3 %copy-start.11 = (bf16[512,1024]{1,0:T(8,128)(2,1)S(1)}, bf16[512,1024]{1,0:T(8,128)(2,1)}, u32[]{:S(2)}) copy-start(bf16[512,1024]{1,0:T(8,128)(2,1)} %param.10) | copy-start | bytes 3145732
  31.7 2.2 %copy-start.3 = (f32[512,8,128]{0,2,1:T(8,128)S(1)}, f32[512,8,128]{0,2,1:T(8,128)}, u32[]{:S(2)}) copy-start(f32[512,8,128]{0,2,1:T(8,128)} %copy.55) | copy-start | bytes 6291460
  31.7 2.6 %copy-start.5 = (bf16[512,1024]{1,0:T(8,128)(2,1)S(1)}, bf16[512,1024]{1,0:T(8,128)(2,1)}, u32[]{:S(2)}) copy-start(bf16[512,1024]{1,0:T(8,128)(2,1)} %param.11) | copy-start | bytes 3145732
  33.9 1.7 %copy-start.1 = (f32[512,8,128]{0,2,1:T(8,128)S(1)}, f32[512,8,128]{0,2,1:T(8,128)}, u32[]{:S(2)}) copy-start(f32[512,8,128]{0,2,1:T(8,128)} %copy.57) | copy-start | bytes 6291460
  33.9 1.7 %copy-start.7 = (f32[1024]{0:T(1024)S(1)}, f32[1024]{0:T(1024)}, u32[]{:S(2)}) copy-start(f32[1024]{0:T(1024)} %param.16) | copy-start | bytes 12292
  33.9 1.7 %copy-start.8 = (f32[1024]{0:T(1024)S(1)}, f32[1024]{0:T(1024)}, u32[]{:S(2)}) copy-start(f32[1024]{0:T(1024)} %param.18) | copy-start | bytes 12292
  33.9 1.7 %copy-start.14 = (f32[1024]{0:T(1024)S(1)}, f32[1024]{0:T(1024)}, u32[]{:S(2)}) copy-start(f32[1024]{0:T(1024)} %param.17) | copy-start | bytes 12292
  33.9 1.7 %copy-start.15 = (f32[1024]{0:T(1024)S(1)}, f32[1024]{0:T(1024)}, u32[]{:S(2)}) copy-start(f32[1024]{0:T(1024)} %param.19) | copy-start | bytes 12292
  133.9 4.8 %copy-start.2 = (f32[512,8,128]{0,2,1:T(8,128)S(1)}, f32[512,8,128]{0,2,1:T(8,128)}, u32[]{:S(2)}) copy-start(f32[512,8,128]{0,2,1:T(8,128)} %copy.57) | copy-start | bytes 6291460
  133.9 4.8 %copy-start.4 = (f32[512,8,128]{0,2,1:T(8,128)S(1)}, f32[512,8,128]{0,2,1:T(8,128)}, u32[]{:S(2)}) copy-start(f32[512,8,128]{0,2,1:T(8,128)} %copy.55) | copy-start | bytes 6291460
  133.9 4.8 %copy-start.13 = (f32[8,128,128]{2,1,0:T(8,128)S(1)}, f32[8,128,128]{2,1,0:T(8,128)}, u32[]{:S(2)}) copy-start(f32[8,128,128]{2,1,0:T(8,128)} %get-tuple-element.10) | copy-start | bytes 1572868
  141.3 1.4 copy-start.6
  141.3 1.4 copy-start.12
  142.6 1.6 %copy-start.9 = (bf16[1024,1024]{1,0:T(8,128)(2,1)S(1)}, bf16[1024,1024]{1,0:T(8,128)(2,1)}, u32[]{:S(2)}) copy-start(bf16[1024,1024]{1,0:T(8,128)(2,1)} %param.13) | copy-start | bytes 6291460
  145.5 1.6 %copy-start.10 = (bf16[1024,1024]{1,0:T(8,128)(2,1)S(1)}, bf16[1024,1024]{1,0:T(8,128)(2,1)}, u32[]{:S(2)}) copy-start(bf16[1024,1024]{1,0:T(8,128)(2,1)} %param.15) | copy-start | bytes 6291460
Sparse Core Ops, SparseCore 0:
  37.7 96.1 all-reduce.2
where the time goes:
time: 157 us; the launch traced here: 156 us
  waiting for transfers between devices  60.4 us (38%)
  blocking collectives  35.9 us (23%)
  matrix products  24.6 us (16%)
  between operations  14.3 us (9%)
  local copies, waits for them, and re-layouts  12.5 us (8%)
  other arithmetic  8.47 us (5%)
    psum x1, waiting for transfers between devices, body(): kv_sum = lax.psum(kv_local, 'dx')  60.4 us
    psum x1, blocking collectives, body(): total = lax.psum(own_count, 'dx')  35.9 us
    reshape x2, local copies, waits for them, and re-layouts, head_norm(): grouped = raw.reshape(raw.shape[0], heads, -1)  5.92 us
    unnamed x34, local copies, waits for them, and re-layouts  4.87 us
    dot_general x1, matrix products, body(): jnp.einsum('nhi,hij->nhj', keys, dgram, preferred_element_type=jnp.float32)  4.81 us
    reduce_sum x2, other arithmetic, head_norm(): center = grouped - jnp.mean(grouped, axis=2, keepdims=True)  4.51 us
    dot_general x1, matrix products, body(): jnp.dot(points, w_query, preferred_element_type=jnp.float32)  4.15 us
    dot_general x1, matrix products, body(): jnp.dot(points, w_value, preferred_element_type=jnp.float32)  3.3 us
  transfers between devices with their start and end apart: 1, of which 1 were waited for; matrix products, arithmetic and copies ran while one was open for 0% of the time, Pallas kernels for 0%

commit v1 on v0

--- a/solution.py
+++ b/solution.py
@@ -5,6 +5,15 @@
 
 HEADS = 8
 eps = 1e-05
+
+
+def doubling_sum(block, axis):
+    size = lax.axis_size(axis)
+    total, far = (block, 1)
+    while far < size:
+        total = total + lax.ppermute(total, axis, [(i, i ^ far) for i in range(size)])
+        far = 2 * far
+    return total
 
 
 def head_norm(raw, heads):
@@ -42,7 +51,7 @@
     ).astype(jnp.bfloat16)
     kv_local = jnp.einsum("nhi,nhj->hij", keys, values, preferred_element_type=jnp.float32)
     cot = cotangent.reshape(rows, heads, -1)
-    kv_sum = lax.psum(kv_local, "dx")
+    kv_sum = doubling_sum(kv_local, "dx")
     query = jnp.dot(points, w_query, preferred_element_type=jnp.float32).astype(jnp.bfloat16)
     masked_query = (query * live.astype(jnp.bfloat16)).reshape(rows, heads, -1)
     qdy_local = jnp.einsum("nhi,nhj->hij", masked_query, cot, preferred_element_type=jnp.float32)

time: 157 us -> 180 us (1.15)
  waiting for transfers between devices: 60.4 us -> 82.5 us
    ppermute x0 -> x4, waiting for transfers between devices: none -> 48.5 us  [doubling_sum(): lax.ppermute(total, axis, [(i, i ^ far) for i in range(size)])]
    psum x1, waiting for transfers between devices: 60.4 us -> 33.9 us  [body(): qdy_sum = lax.psum(qdy_local, 'dx')]
    unnamed x34 -> x30, local copies, waits for them, and re-layouts: 4.87 us -> 4.33 us
  transfers between devices with their start and end apart: 1 -> 5, of which waited for: 1 -> 4; matrix products, arithmetic and copies ran while one was open for 0% -> 17% of each run, Pallas kernels for 0% -> 0%
where the time goes in v1:
time: 180 us; the launch traced here: 179 us
  waiting for transfers between devices  82.5 us (46%)
  blocking collectives  35.9 us (20%)
  matrix products  24.5 us (14%)
  between operations  14.5 us (8%)
  local copies, waits for them, and re-layouts  11.9 us (7%)
  other arithmetic  8.67 us (5%)
    ppermute x4, waiting for transfers between devices, doubling_sum(): lax.ppermute(total, axis, [(i, i ^ far) for i in range(size)])  48.5 us
    psum x1, blocking collectives, body(): total = lax.psum(own_count, 'dx')  35.9 us
    psum x1, waiting for transfers between devices, body(): qdy_sum = lax.psum(qdy_local, 'dx')  33.9 us
    reshape x2, local copies, waits for them, and re-layouts, head_norm(): grouped = raw.reshape(raw.shape[0], heads, -1)  5.92 us
    dot_general x1, matrix products, body(): jnp.einsum('nhi,hij->nhj', keys, dgram, preferred_element_type=jnp.float32)  4.71 us
    reduce_sum x2, other arithmetic, head_norm(): center = grouped - jnp.mean(grouped, axis=2, keepdims=True)  4.53 us
    unnamed x30, local copies, waits for them, and re-layouts  4.33 us
    dot_general x1, matrix products, body(): jnp.dot(points, w_query, preferred_element_type=jnp.float32)  4.15 us
  transfers between devices with their start and end apart: 5, of which 4 were waited for; matrix products, arithmetic and copies ran while one was open for 17% of the time, Pallas kernels for 0%

profile of v1, /device:TPU:0, one launch (start us, length us, event | category | flops | bytes accessed | tf_op | source)
XLA Modules:
  0.0 179.4 jit_solution(9983139068857051653)
XLA Ops:
  7.4 4.1 %fusion.8 = bf16[512,1024]{1,0:T(8,128)(2,1)} fusion(bf16[512,1024]{1,0:T(8,128)(2,1)} %param.10, bf16[1024,1024]{1,0:T(8,128)(2,1)} %param.13, bf16[512]{0:T(512)(128)(2,1)S(1)} %fusion.16), kind=kOutput, calls=%fused_computation.25 | convolution fusion | flops 1074790400 | bytes 4195328 | tf_op jit(solution)/shard_map/dot_general | solution.py:55
  11.5 1.5 copy.71
  13.0 2.5 %fusion.9 = f32[8,128,128]{2,1,0:T(8,128)} fusion(bf16[512,8,128]{0,2,1:T(8,128)(2,1)S(1)} %bitcast.73, bf16[512,1024]{1,0:T(8,128)(2,1)} %param.11), kind=kOutput, calls=%fused_computation.26 | convolution fusion | flops 134217728 | bytes 2621440 | tf_op jit(solution)/shard_map/nhi,nhj->hij/dot_general | solution.py:57
  15.5 0.0 all-reduce.2.cloned.1.call-update
  15.5 3.2 %convolution_bitcast_fusion = f32[64,8,8,128]{3,1,2,0:T(8,128)S(1)} fusion(bf16[512,1024]{1,0:T(8,128)(2,1)} %param.10, bf16[1024,1024]{1,0:T(8,128)(2,1)} %param.15), kind=kOutput, calls=%fused_computation.22 | convolution fusion | flops 1073741824 | bytes 5242880 | tf_op jit(solution)/shard_map/dot_general | solution.py:44
  18.7 1.8 copy.74
  20.4 3.0 %copy.59 = f32[512,8,128]{0,2,1:T(8,128)} copy(f32[512,8,128]{2,1,0:T(8,128)} %bitcast.71) | data formatting | bytes 4194304 | tf_op jit(solution)/shard_map/reshape | solution.py:20
  23.4 2.3 %reduce_sum.74 = f32[512,8]{1,0:T(8,128)S(1)} reduce(f32[512,8,128]{2,1,0:T(8,128)} %bitcast.72, f32[]{:T(128)} %constant.11.clone.1), dimensions={2}, to_apply=%region_2.0 | reduce | flops 520192 | bytes 2113540 | tf_op jit(solution)/shard_map/reduce_sum | solution.py:21
  25.8 1.2 convolution_bitcast_fusion.1
  27.0 1.8 copy.73
  28.8 2.9 %copy.57 = f32[512,8,128]{0,2,1:T(8,128)} copy(f32[512,8,128]{2,1,0:T(8,128)} %bitcast.69) | data formatting | bytes 4194304 | tf_op jit(solution)/shard_map/reshape | solution.py:20
  31.7 2.2 %reduce_sum.72 = f32[512,8]{1,0:T(8,128)S(1)} reduce(f32[512,8,128]{2,1,0:T(8,128)} %bitcast.70, f32[]{:T(128)} %constant.11.clone.1), dimensions={2}, to_apply=%region_0.0 | reduce | flops 520192 | bytes 2113540 | tf_op jit(solution)/shard_map/reduce_sum | solution.py:21
  34.0 0.1 copy.58
  34.1 0.1 copy.56
  34.2 0.0 copy-start.1
  34.2 0.0 copy-start.6
  34.2 0.0 copy-start.7
  34.2 0.0 copy-start.12
  34.2 0.0 copy-start.13
  34.3 2.1 %multiply_reduce_fusion = f32[512,8]{0,1:T(8,128)S(1)} fusion(f32[512,8,128]{0,2,1:T(8,128)} %copy.59, f32[512,8]{0,1:T(8,128)S(1)} %broadcast_multiply_fusion.4), kind=kLoop, calls=%fused_computation.17 | loop fusion | flops 1568768 | bytes 2129920 | tf_op jit(solution)/shard_map/reduce_sum | solution.py:22
  36.3 0.1 copy-done.1
  36.4 0.3 multiply_reduce_fusion.1
  36.8 0.3 copy-done.3
  37.1 1.1 fusion.18
  38.2 0.5 collective-permute-start
  38.8 35.9 %psum.14 = f32[]{:T(128)} all-reduce(f32[]{:T(128)S(6)} %convert_element_type.64), channel_id=1, replica_groups=mesh['group'=2,'dx'=16] {'dx'}, use_global_device_ids=true, to_apply=%region_4.0 | all-reduce | flops 1 | bytes 8 | tf_op jit(solution)/shard_map/psum | solution.py:41
  74.6 33.9 %all-reduce.2.cloned.1.call-done = f32[8,128,128]{2,1,0:T(8,128)} async-done(((f32[8,128,128]{2,1,0:T(8,128)}), f32[8,128,128]{2,1,0:T(8,128)}) %all-reduce.2.cloned.1.call-update) | async-done | bytes 524304 | tf_op jit(solution)/shard_map/psum | solution.py:58
  108.5 4.7 %bitcast_reduce_fusion = (f32[512,8]{0,1:T(8,128)S(1)}, f32[512,8]{0,1:T(8,128)S(1)}, f32[8,128,512]{2,1,0:T(8,128)S(1)}) fusion(f32[8,128]{1,0:T(8,128)S(1)} %bitcast.77, f32[512,8]{0,1:T(8,128)S(1)} %get-tuple-element.11, f32[512,8,128]{0,2,1:T(8,128)} %copy.59, f32[512,8]{0,1:T(8,128)S(1)} %broadcast_multiply_fusion.4, f32[512,8,128]{0,2,1:T(8,128)} %copy.57, ...), kind=kOutput, calls=%fused_computation.2 | convolution fusion | flops 140763136 | bytes 6928388 | tf_op jit(solution)/shard_map/nhi,hij->nhj/dot_general | solution.py:67
  113.3 1.6 bitcast_reduce_fusion.1
  114.9 0.1 add.66
  115.0 0.7 collective-permute-start.1
  115.6 13.7 %collective-permute-done.1 = f32[8,128,128]{2,1,0:T(8,128)S(1)} collective-permute-done((f32[8,128,128]{2,1,0:T(8,128)S(1)}, f32[8,128,128]{2,1,0:T(8,128)S(1)}, u32[]{:S(2)}, u32[]{:S(2)}) %collective-permute-start.1) | collective-permute-done | bytes 524320 | tf_op jit(solution)/shard_map/ppermute | solution.py:14
  129.3 0.1 add.67
  129.4 0.3 collective-permute-start.2
  129.7 0.8 fusion.2
  130.5 12.5 %collective-permute-done.2 = f32[8,128,128]{2,1,0:T(8,128)S(1)} collective-permute-done((f32[8,128,128]{2,1,0:T(8,128)S(1)}, f32[8,128,128]{2,1,0:T(8,128)S(1)}, u32[]{:S(2)}, u32[]{:S(2)}) %collective-permute-start.2) | collective-permute-done | bytes 524320 | tf_op jit(solution)/shard_map/ppermute | solution.py:14
  143.0 0.1 add.68
  143.0 0.1 collective-permute-start.3
  143.1 0.8 fusion.6
  143.9 0.0 copy-start.5
  143.9 1.3 fusion.21
  145.2 0.0 copy-start.8
  145.2 22.4 %collective-permute-done.3 = f32[8,128,128]{2,1,0:T(8,128)S(1)} collective-permute-done((f32[8,128,128]{2,1,0:T(8,128)S(1)}, f32[8,128,128]{2,1,0:T(8,128)S(1)}, u32[]{:S(2)}, u32[]{:S(2)}) %collective-permute-start.3) | collective-permute-done | bytes 524320 | tf_op jit(solution)/shard_map/ppermute | solution.py:14
  167.6 1.1 multiply_convert_fusion
  168.7 0.0 copy-start.9
  168.7 1.3 fusion.20
  170.0 0.3 copy-done.9
  170.3 2.3 %add_convert_fusion = bf16[512,1024]{1,0:T(8,128)(2,1)} fusion(f32[512,1024]{1,0:T(8,128)S(1)} %fusion.20, f32[512,1024]{1,0:T(8,128)S(1)} %fusion.21, bf16[512,1024]{0,1:T(8,128)(2,1)S(1)} %bitcast.74, bf16[1024,1024]{1,0:T(8,128)(2,1)S(1)} %copy-done.9), kind=kOutput, calls=%fused_computation.14 | convolution fusion | flops 1075314688 | bytes 8388608 | tf_op jit(solution)/shard_map/dot_general | solution.py:72
  (28 shorter events, 0.1 us)
Async XLA Ops:
  6.5 19.2 %copy-start = (bf16[1024,1024]{1,0:T(8,128)(2,1)S(1)}, bf16[1024,1024]{1,0:T(8,128)(2,1)}, u32[]{:S(2)}) copy-start(bf16[1024,1024]{1,0:T(8,128)(2,1)} %param.14) | copy-start | bytes 6291460
  6.5 102.0 %all-reduce.2.cloned.1.call-start = ((), (), s32[]{:S(2)}) async-start(), calls=%async_computation | async-start | bytes 1048576 | tf_op jit(solution)/shard_map/psum | solution.py:58
  23.4 2.3 %copy-start.10 = (bf16[512,1024]{1,0:T(8,128)(2,1)S(1)}, bf16[512,1024]{1,0:T(8,128)(2,1)}, u32[]{:S(2)}) copy-start(bf16[512,1024]{1,0:T(8,128)(2,1)} %param.10) | copy-start | bytes 3145732
  34.2 2.3 %copy-start.1 = (f32[512,8,128]{0,2,1:T(8,128)S(1)}, f32[512,8,128]{0,2,1:T(8,128)}, u32[]{:S(2)}) copy-start(f32[512,8,128]{0,2,1:T(8,128)} %copy.57) | copy-start | bytes 6291460
  34.2 2.9 %copy-start.3 = (f32[512,8,128]{0,2,1:T(8,128)S(1)}, f32[512,8,128]{0,2,1:T(8,128)}, u32[]{:S(2)}) copy-start(f32[512,8,128]{0,2,1:T(8,128)} %copy.59) | copy-start | bytes 6291460
  34.2 2.9 %copy-start.6 = (f32[1024]{0:T(1024)S(1)}, f32[1024]{0:T(1024)}, u32[]{:S(2)}) copy-start(f32[1024]{0:T(1024)} %param.18) | copy-start | bytes 12292
  34.2 2.9 %copy-start.7 = (f32[1024]{0:T(1024)S(1)}, f32[1024]{0:T(1024)}, u32[]{:S(2)}) copy-start(f32[1024]{0:T(1024)} %param.16) | copy-start | bytes 12292
  34.2 2.8 %copy-start.12 = (f32[1024]{0:T(1024)S(1)}, f32[1024]{0:T(1024)}, u32[]{:S(2)}) copy-start(f32[1024]{0:T(1024)} %param.17) | copy-start | bytes 12292
  34.2 2.8 %copy-start.13 = (f32[1024]{0:T(1024)S(1)}, f32[1024]{0:T(1024)}, u32[]{:S(2)}) copy-start(f32[1024]{0:T(1024)} %param.19) | copy-start | bytes 12292
  38.2 76.7 %collective-permute-start = (f32[8,128,128]{2,1,0:T(8,128)S(1)}, f32[8,128,128]{2,1,0:T(8,128)S(1)}, u32[]{:S(2)}, u32[]{:S(2)}) collective-permute-start(f32[8,128,128]{2,1,0:T(8,128)S(1)} %fusion.18), channel_id=1, source_target_pairs={{0,1},{1,0},{2,3},{3,2},{4,5},{5,4},{6,7},{7,6},{8,9},{9,8},{10,11... | collective-permute-start | bytes 1572872 | tf_op jit(solution)/shard_map/ppermute | solution.py:14
  108.5 4.7 %copy-start.2 = (f32[512,8,128]{0,2,1:T(8,128)S(1)}, f32[512,8,128]{0,2,1:T(8,128)}, u32[]{:S(2)}) copy-start(f32[512,8,128]{0,2,1:T(8,128)} %copy.57) | copy-start | bytes 6291460
  108.5 4.7 %copy-start.4 = (f32[512,8,128]{0,2,1:T(8,128)S(1)}, f32[512,8,128]{0,2,1:T(8,128)}, u32[]{:S(2)}) copy-start(f32[512,8,128]{0,2,1:T(8,128)} %copy.59) | copy-start | bytes 6291460
  108.5 4.7 %copy-start.11 = (f32[8,128,128]{2,1,0:T(8,128)S(1)}, f32[8,128,128]{2,1,0:T(8,128)}, u32[]{:S(2)}) copy-start(f32[8,128,128]{2,1,0:T(8,128)} %all-reduce.2.cloned.1.call-done) | copy-start | bytes 1572868
  115.0 14.4 %collective-permute-start.1 = (f32[8,128,128]{2,1,0:T(8,128)S(1)}, f32[8,128,128]{2,1,0:T(8,128)S(1)}, u32[]{:S(2)}, u32[]{:S(2)}) collective-permute-start(f32[8,128,128]{2,1,0:T(8,128)S(1)} %add.66), channel_id=1, source_target_pairs={{0,2},{1,3},{2,0},{3,1},{4,6},{5,7},{6,4},{7,5},{8,10},{9,11},{10,... | collective-permute-start | bytes 1572872 | tf_op jit(solution)/shard_map/ppermute | solution.py:14
  129.4 13.6 %collective-permute-start.2 = (f32[8,128,128]{2,1,0:T(8,128)S(1)}, f32[8,128,128]{2,1,0:T(8,128)S(1)}, u32[]{:S(2)}, u32[]{:S(2)}) collective-permute-start(f32[8,128,128]{2,1,0:T(8,128)S(1)} %add.67), channel_id=1, source_target_pairs={{0,4},{1,5},{2,6},{3,7},{4,0},{5,1},{6,2},{7,3},{8,12},{9,13},{10,... | collective-permute-start | bytes 1572872 | tf_op jit(solution)/shard_map/ppermute | solution.py:14
  143.0 24.6 %collective-permute-start.3 = (f32[8,128,128]{2,1,0:T(8,128)S(1)}, f32[8,128,128]{2,1,0:T(8,128)S(1)}, u32[]{:S(2)}, u32[]{:S(2)}) collective-permute-start(f32[8,128,128]{2,1,0:T(8,128)S(1)} %add.68), channel_id=1, source_target_pairs={{0,8},{1,9},{2,10},{3,11},{4,12},{5,13},{6,14},{7,15},{8,0},{9,1},... | collective-permute-start | bytes 1572872 | tf_op jit(solution)/shard_map/ppermute | solution.py:14
  143.9 23.7 %copy-start.5 = (bf16[512,1024]{1,0:T(8,128)(2,1)S(1)}, bf16[512,1024]{1,0:T(8,128)(2,1)}, u32[]{:S(2)}) copy-start(bf16[512,1024]{1,0:T(8,128)(2,1)} %param.11) | copy-start | bytes 3145732
  145.2 23.5 %copy-start.8 = (bf16[1024,1024]{1,0:T(8,128)(2,1)S(1)}, bf16[1024,1024]{1,0:T(8,128)(2,1)}, u32[]{:S(2)}) copy-start(bf16[1024,1024]{1,0:T(8,128)(2,1)} %param.13) | copy-start | bytes 6291460
  168.7 1.6 copy-start.9
Sparse Core Ops, SparseCore 0:
  15.6 92.8 all-reduce.1
